TPU v7x, 32 devices: a whole 2x2x4 slice. The times are simulated.
32 devices in a mesh: grp: 2 (over x), ep: 16 (over z, y, core).
Axes of the slice: x: 2, y: 2, z: 4, core: 2. Of those that a mesh axis runs over, the one named last changes fastest.
Arguments:
- tokens_one: bfloat16 [1024, 2048], P(('grp', 'ep')), may hold values from -6 to 6
- routes_one: int32 [1024, 6], P(('grp', 'ep')), may hold values from 0 to 15, all different within a row; in each aligned block of 32 rows (0 to 31, 32 to 63, ...) at most 18 rows name the same one
- gates_one: bfloat16 [1024, 6], P(('grp', 'ep')), may hold values from 0.049804688 to 0.3984375
- tokens_two: bfloat16 [1024, 2048], P(('grp', 'ep')), may hold values from -6 to 6
- routes_two: int32 [1024, 6], P(('grp', 'ep')), may hold values from 0 to 15, all different within a row; in each aligned block of 32 rows (0 to 31, 32 to 63, ...) at most 18 rows name the same one
- gates_two: bfloat16 [1024, 6], P(('grp', 'ep')), may hold values from 0.049804688 to 0.3984375
- old_table: int32 [16], replicated, may hold values from 0 to 15, each once
- new_table: int32 [16], replicated, may hold values from 0 to 15, each once
- gate_up: bfloat16 [16, 2048, 1408], P('ep'), may hold values from -0.125 to 0.125
- down_proj: bfloat16 [16, 704, 2048], P('ep'), may hold values from -0.21875 to 0.21875
- norm_gain: bfloat16 [2048], replicated, may hold values from 0.099609375 to 1.8984375
- kv_weight: bfloat16 [2048, 1024], P(None, 'grp'), may hold values from -0.125 to 0.125
Outputs:
- hidden_one: bfloat16 [1024, 2048], P(('grp', 'ep'))
- kv_one: bfloat16 [1024, 1024], P(('grp', 'ep'))
- hidden_two: bfloat16 [1024, 2048], P(('grp', 'ep'))
- kv_two: bfloat16 [1024, 1024], P(('grp', 'ep'))
- gate_up_new: bfloat16 [16, 2048, 1408], P('ep', 'grp')
- down_proj_new: bfloat16 [16, 704, 2048], P('ep', None, 'grp')
Inputs may be any that keep to these rules, and one draw needn't show every extreme that they name: `routes_one`: each row names 6 different slots; among the rows of one device no slot is named by more than 18 routes, a bound that some block reaches. `routes_two`: each row names 6 different slots; among the rows of one device no slot is named by more than 18 routes, a bound that some block reaches. `old_table`: each expert appears once. `new_table`: each expert appears once.
All inputs are finite; a program needn't handle non-finite values.
Results may differ from a plain program's by a relative error of at most 0.006.
Values may be sent and summed in bfloat16 or wider, within the bound.
No kernel may reach another device: no remote copies, remote signals or barrier semaphores. Data moves between devices by JAX's collectives and lax.ppermute only.
A program may use at most 128 MiB of HBM per device.

v0:
```python
import jax
import jax.numpy as jnp
from jax import lax
from jax.sharding import PartitionSpec as P

TOP = 6


def expert_ffn(activation, weight_in, weight_out):
    inner = weight_out.shape[0]
    joined = jnp.dot(activation, weight_in, preferred_element_type=jnp.float32)
    gate_part = joined[:, :inner]
    upward = joined[:, inner:]
    hidden = (jax.nn.silu(gate_part) * upward).astype(jnp.bfloat16)
    return jnp.dot(hidden, weight_out, preferred_element_type=jnp.float32).astype(jnp.bfloat16)


def dispatch_plan(owners, ep_size, capacity):
    flattened = owners.reshape(-1)
    matches = (
        flattened[:, None] == lax.broadcasted_iota(jnp.int32, (flattened.shape[0], ep_size), 1)
    ).astype(jnp.int32)
    earlier = jnp.cumsum(matches, axis=0) - matches
    ranking = jnp.sum(earlier * matches, axis=1)
    return flattened * capacity + ranking


def routed_layer(tokens, owners, gate_share, weight_in, weight_out):
    ep_size = lax.axis_size("ep")
    rows_here = tokens.shape[0]
    features = tokens.shape[1]
    capacity = 3 * rows_here * TOP // (2 * ep_size)
    targets = dispatch_plan(owners, ep_size, capacity)
    senders = jnp.arange(rows_here * TOP, dtype=jnp.int32) // TOP
    packed = (
        jnp.zeros((ep_size * capacity, features), jnp.bfloat16).at[targets].set(tokens[senders])
    )
    packed = packed.reshape(ep_size, capacity, features)
    arrived = lax.all_to_all(packed, "ep", split_axis=0, concat_axis=0, tiled=True)
    sources, slot_count, columns = arrived.shape
    result = expert_ffn(arrived.reshape(sources * slot_count, columns), weight_in, weight_out)
    returned = lax.all_to_all(
        result.reshape(sources, slot_count, columns), "ep", split_axis=0, concat_axis=0, tiled=True
    )
    outputs = returned.reshape(ep_size * capacity, features)[targets].reshape(
        rows_here, TOP, features
    )
    mixture = jnp.einsum("tk,tkd->td", gate_share.astype(jnp.float32), outputs.astype(jnp.float32))
    return (tokens.astype(jnp.float32) + mixture).astype(jnp.bfloat16)


def rms_norm(hidden, norm_gain):
    values = hidden.astype(jnp.float32)
    inverse_rms = lax.rsqrt(jnp.mean(values * values, axis=-1, keepdims=True) + 1e-06)
    return (values * inverse_rms * norm_gain.astype(jnp.float32)).astype(jnp.bfloat16)


def local(
    tokens_one,
    routes_one,
    gates_one,
    tokens_two,
    routes_two,
    gates_two,
    old_table,
    new_table,
    gate_up,
    down_proj,
    norm_gain,
    kv_weight,
):
    local_in = gate_up[0]
    local_out = down_proj[0]
    ep_size = lax.axis_size("ep")
    grp_size = lax.axis_size("grp")
    numbers = jnp.arange(ep_size, dtype=jnp.int32)
    held_where = (old_table[:, None] == numbers[None, :]).astype(jnp.int32)
    old_inverse = jnp.sum(held_where * numbers[:, None], axis=0)
    wanted = (new_table[:, None] == numbers[None, :]).astype(jnp.int32)
    sources_new = jnp.sum(wanted * old_inverse[None, :], axis=1)
    features = local_in.shape[0]
    inner = local_out.shape[0]
    spread = (
        lax.all_to_all(
            local_in.reshape(ep_size, features // ep_size, 2 * inner),
            "ep",
            split_axis=0,
            concat_axis=0,
            tiled=True,
        ),
        lax.all_to_all(
            local_out.reshape(ep_size, inner // ep_size, features),
            "ep",
            split_axis=0,
            concat_axis=0,
            tiled=True,
        ),
    )
    regrouped_in = spread[0][sources_new]
    regrouped_out = spread[1][sources_new]
    collected = (
        lax.all_to_all(regrouped_in, "ep", split_axis=0, concat_axis=0, tiled=True),
        lax.all_to_all(regrouped_out, "ep", split_axis=0, concat_axis=0, tiled=True),
    )
    moved_in = collected[0].reshape(features, 2 * inner)
    moved_out = collected[1].reshape(inner, features)
    hidden_one = routed_layer(tokens_one, routes_one, gates_one, local_in, local_out)
    hidden_two = routed_layer(tokens_two, routes_two, gates_two, moved_in, moved_out)
    part_rows = features // grp_size
    part_start = lax.axis_index("grp") * part_rows
    gate_up_new = lax.dynamic_slice_in_dim(moved_in, part_start, part_rows, 0)[None]
    down_proj_new = lax.dynamic_slice_in_dim(moved_out, part_start, part_rows, 1)[None]
    normed = jnp.concatenate(
        [rms_norm(hidden_one, norm_gain), rms_norm(hidden_two, norm_gain)], axis=0
    )
    projected = jnp.dot(
        normed,
        lax.all_gather(kv_weight, "grp", axis=1, tiled=True),
        preferred_element_type=jnp.float32,
    ).astype(jnp.bfloat16)
    rows_here = tokens_one.shape[0]
    return (
        hidden_one,
        projected[:rows_here],
        hidden_two,
        projected[rows_here:],
        gate_up_new,
        down_proj_new,
    )


def solution(mesh):
    return jax.shard_map(
        local,
        mesh=mesh,
        in_specs=(
            P(("grp", "ep"), None),
            P(("grp", "ep"), None),
            P(("grp", "ep"), None),
            P(("grp", "ep"), None),
            P(("grp", "ep"), None),
            P(("grp", "ep"), None),
            P(),
            P(),
            P("ep", None, None),
            P("ep", None, None),
            P(),
            P(None, "grp"),
        ),
        out_specs=(
            P(("grp", "ep"), None),
            P(("grp", "ep"), None),
            P(("grp", "ep"), None),
            P(("grp", "ep"), None),
            P("ep", "grp", None),
            P("ep", None, "grp"),
        ),
        check_vma=False,
    )
```

profile of v0, /device:TPU:13, one launch (start us, length us, event | category | flops | bytes accessed | tf_op | source)
XLA Modules:
  0.0 609.7 jit_solution(7573746176360497464)
XLA Ops:
  9.9 5.3 scatter_custom_fusion.1
  16.6 6.7 %all-to-all-start.2 = ((bf16[16,18,2048]{2,1,0:T(8,128)(2,1)}), bf16[16,18,2048]{2,1,0:T(8,128)(2,1)S(1)}, u32[]{:S(2)}, u32[]{:S(2)}) async-start(bf16[16,18,2048]{2,1,0:T(8,128)(2,1)} %reshape.215), calls=%async_computation.2 | async-start | bytes 3145728 | tf_op jit(solution)/shard_map/all_to_all | solution.py:39
  24.7 4.6 scatter_custom_fusion
  30.6 28.9 %all-to-all-done.2 = bf16[16,18,2048]{2,1,0:T(8,128)(2,1)S(1)} async-done(((bf16[16,18,2048]{2,1,0:T(8,128)(2,1)}), bf16[16,18,2048]{2,1,0:T(8,128)(2,1)S(1)}, u32[]{:S(2)}, u32[]{:S(2)}) %all-to-all-start.2) | async-done | bytes 1179680 | tf_op jit(solution)/shard_map/all_to_all | solution.py:39
  59.5 4.9 all-to-all-start
  64.4 4.3 reshape_squeeze.7
  68.7 32.0 %all-to-all-done = bf16[16,18,2048]{2,1,0:T(8,128)(2,1)} async-done(((bf16[16,18,2048]{2,1,0:T(8,128)(2,1)}), bf16[16,18,2048]{2,1,0:T(8,128)(2,1)}, u32[]{:S(2)}, u32[]{:S(2)}) %all-to-all-start) | async-done | bytes 1179680 | tf_op jit(solution)/shard_map/all_to_all | solution.py:39
  100.7 74.7 %all_to_all.40 = bf16[16,44,2048]{2,1,0:T(8,128)(2,1)S(1)} all-to-all(bf16[16,44,2048]{2,1,0:T(8,128)(2,1)} %reshape_squeeze.7), channel_id=1, replica_groups=mesh['grp'=2,'ep'=16] {'ep'}, dimensions={0} | all-to-all | bytes 5767168 | tf_op jit(solution)/shard_map/all_to_all | solution.py:91
  175.4 5.3 all-to-all-start.3
  181.0 2.5 gather_fusion.2
  183.5 123.4 %all-to-all-done.3 = bf16[16,128,1408]{2,1,0:T(8,128)(2,1)} async-done(((bf16[16,128,1408]{2,1,0:T(8,128)(2,1)}), bf16[16,128,1408]{2,1,0:T(8,128)(2,1)}, u32[]{:S(2)}, u32[]{:S(2)}) %all-to-all-start.3) | async-done | bytes 5767200 | tf_op jit(solution)/shard_map/all_to_all | solution.py:84
  306.9 4.9 all-to-all-start.6
  311.8 6.4 %gather_fusion.1 = bf16[16,128,1408]{2,1,0:T(8,128)(2,1)} fusion(bf16[16,128,1408]{2,1,0:T(8,128)(2,1)} %all-to-all-done.3, s32[1024]{0:T(1024)S(1)} %pad_clamp_fusion.1), kind=kCustom, calls=%fused_computation.3 | custom fusion | bytes 11534400 | tf_op jit(solution)/shard_map/gather | solution.py:99
  318.1 63.5 %all-to-all-done.6 = bf16[16,44,2048]{2,1,0:T(8,128)(2,1)S(1)} async-done(((bf16[16,44,2048]{2,1,0:T(8,128)(2,1)}), bf16[16,44,2048]{2,1,0:T(8,128)(2,1)S(1)}, u32[]{:S(2)}, u32[]{:S(2)}) %all-to-all-start.6) | async-done | bytes 2883616 | tf_op jit(solution)/shard_map/all_to_all | solution.py:103
  381.7 4.9 all-to-all-start.4
  386.6 2.4 reshape.209
  388.9 5.1 fusion
  394.1 2.2 fusion.4
  396.3 2.4 reshape.210
  398.7 114.1 %all-to-all-done.4 = bf16[16,128,1408]{2,1,0:T(8,128)(2,1)} async-done(((bf16[16,128,1408]{2,1,0:T(8,128)(2,1)}), bf16[16,128,1408]{2,1,0:T(8,128)(2,1)}, u32[]{:S(2)}, u32[]{:S(2)}) %all-to-all-start.4) | async-done | bytes 5767200 | tf_op jit(solution)/shard_map/all_to_all | solution.py:102
  512.7 4.9 all-to-all-start.1
  518.4 2.4 reshape.216
  520.8 2.2 reshape.218
  523.0 5.1 fusion.42
  530.7 23.6 %all-to-all-done.1 = bf16[16,18,2048]{2,1,0:T(8,128)(2,1)} async-done(((bf16[16,18,2048]{2,1,0:T(8,128)(2,1)}), bf16[16,18,2048]{2,1,0:T(8,128)(2,1)}, u32[]{:S(2)}, u32[]{:S(2)}) %all-to-all-start.1) | async-done | bytes 1179680 | tf_op jit(solution)/shard_map/all_to_all | solution.py:42
  554.2 4.6 all-to-all-start.7
  560.7 2.0 gather_fusion
  562.7 2.3 reshape.212
  565.0 1.6 fusion.41
  568.2 3.6 dynamic-slice_bitcast_fusion
  571.8 23.4 %all-to-all-done.7 = bf16[16,18,2048]{2,1,0:T(8,128)(2,1)} async-done(((bf16[16,18,2048]{2,1,0:T(8,128)(2,1)}), bf16[16,18,2048]{2,1,0:T(8,128)(2,1)}, u32[]{:S(2)}, u32[]{:S(2)}) %all-to-all-start.7) | async-done | bytes 1179680 | tf_op jit(solution)/shard_map/all_to_all | solution.py:42
  599.2 3.0 convolution_convert_fusion.1
  (85 shorter events, 18.2 us)
Async XLA Ops:
  16.6 6.7 %copy-start.8 = (s32[32,6]{0,1:T(8,128)S(1)}, s32[32,6]{0,1:T(8,128)}, u32[]{:S(2)}) copy-start(s32[32,6]{0,1:T(8,128)} %param.13) | copy-start | bytes 2308
  16.6 8.1 %copy-start.6 = (bf16[32,2048]{1,0:T(8,128)(2,1)S(1)}, bf16[32,2048]{1,0:T(8,128)(2,1)}, u32[]{:S(2)}) copy-start(bf16[32,2048]{1,0:T(8,128)(2,1)} %param.12) | copy-start | bytes 393220
  16.6 42.9 %all-to-all-start.2 = ((bf16[16,18,2048]{2,1,0:T(8,128)(2,1)}), bf16[16,18,2048]{2,1,0:T(8,128)(2,1)S(1)}, u32[]{:S(2)}, u32[]{:S(2)}) async-start(bf16[16,18,2048]{2,1,0:T(8,128)(2,1)} %reshape.215), calls=%async_computation.2 | async-start | bytes 3145728 | tf_op jit(solution)/shard_map/all_to_all | solution.py:39
  59.5 9.2 %copy-start.2 = (bf16[16,18,2048]{2,1,0:T(8,128)(2,1)}, bf16[16,18,2048]{2,1,0:T(8,128)(2,1)S(1)}, u32[]{:S(2)}) copy-start(bf16[16,18,2048]{2,1,0:T(8,128)(2,1)S(1)} %all-to-all-done.2) | copy-start | bytes 3538948
  59.5 41.2 %all-to-all-start = ((bf16[16,18,2048]{2,1,0:T(8,128)(2,1)}), bf16[16,18,2048]{2,1,0:T(8,128)(2,1)}, u32[]{:S(2)}, u32[]{:S(2)}) async-start(bf16[16,18,2048]{2,1,0:T(8,128)(2,1)} %reshape.208), calls=%async_computation | async-start | bytes 3145728 | tf_op jit(solution)/shard_map/all_to_all | solution.py:39
  175.3 5.3 copy-start.12
  175.3 5.4 copy-start.13
  175.4 131.5 %all-to-all-start.3 = ((bf16[16,128,1408]{2,1,0:T(8,128)(2,1)}), bf16[16,128,1408]{2,1,0:T(8,128)(2,1)}, u32[]{:S(2)}, u32[]{:S(2)}) async-start(bf16[16,128,1408]{2,1,0:T(8,128)(2,1)} %bitcast.68), calls=%async_computation.3 | async-start | bytes 11534336 | tf_op jit(solution)/shard_map/all_to_all | solution.py:84
  306.9 74.8 %all-to-all-start.6 = ((bf16[16,44,2048]{2,1,0:T(8,128)(2,1)}), bf16[16,44,2048]{2,1,0:T(8,128)(2,1)S(1)}, u32[]{:S(2)}, u32[]{:S(2)}) async-start(bf16[16,44,2048]{2,1,0:T(8,128)(2,1)} %gather_fusion.2), calls=%async_computation.6 | async-start | bytes 6291456 | tf_op jit(solution)/shard_map/all_to_all | solution.py:103
  381.7 131.1 %all-to-all-start.4 = ((bf16[16,128,1408]{2,1,0:T(8,128)(2,1)}), bf16[16,128,1408]{2,1,0:T(8,128)(2,1)}, u32[]{:S(2)}, u32[]{:S(2)}) async-start(bf16[16,128,1408]{2,1,0:T(8,128)(2,1)} %gather_fusion.1), calls=%async_computation.4 | async-start | bytes 11534336 | tf_op jit(solution)/shard_map/all_to_all | solution.py:102
  388.9 5.1 copy-start.3
  512.7 41.5 %all-to-all-start.1 = ((bf16[16,18,2048]{2,1,0:T(8,128)(2,1)}), bf16[16,18,2048]{2,1,0:T(8,128)(2,1)}, u32[]{:S(2)}, u32[]{:S(2)}) async-start(bf16[16,18,2048]{2,1,0:T(8,128)(2,1)} %reshape.210), calls=%async_computation.1 | async-start | bytes 3145728 | tf_op jit(solution)/shard_map/all_to_all | solution.py:42
  517.6 81.5 %all-gather.2.cloned.1.call-start = ((), (), s32[]{:S(2)}) async-start(), calls=%async_computation.8 | async-start | bytes 6291456 | tf_op jit(solution)/shard_map/all_gather | solution.py:118
  523.0 5.1 copy-start
  530.7 28.2 %copy-start.10 = (bf16[32,6]{0,1:T(8,128)(2,1)S(1)}, bf16[32,6]{0,1:T(8,128)(2,1)}, u32[]{:S(2)}) copy-start(bf16[32,6]{0,1:T(8,128)(2,1)} %param.17) | copy-start | bytes 1156
  530.7 28.3 %copy-start.11 = (bf16[32,6]{0,1:T(8,128)(2,1)S(1)}, bf16[32,6]{0,1:T(8,128)(2,1)}, u32[]{:S(2)}) copy-start(bf16[32,6]{0,1:T(8,128)(2,1)} %param.14) | copy-start | bytes 1156
  530.7 28.4 %copy-start.9 = (bf16[2048]{0:T(1024)(128)(2,1)S(1)}, bf16[2048]{0:T(1024)(128)(2,1)}, u32[]{:S(2)}) copy-start(bf16[2048]{0:T(1024)(128)(2,1)} %param.22) | copy-start | bytes 12292
  554.2 40.9 %all-to-all-start.7 = ((bf16[16,18,2048]{2,1,0:T(8,128)(2,1)}), bf16[16,18,2048]{2,1,0:T(8,128)(2,1)}, u32[]{:S(2)}, u32[]{:S(2)}) async-start(bf16[16,18,2048]{2,1,0:T(8,128)(2,1)} %reshape.219), calls=%async_computation.7 | async-start | bytes 3145728 | tf_op jit(solution)/shard_map/all_to_all | solution.py:42
  562.7 4.2 copy-start.1
  566.9 32.1 %copy-start.4 = (bf16[32,2048]{1,0:T(8,128)(2,1)}, bf16[32,2048]{1,0:T(8,128)(2,1)S(1)}, u32[]{:S(2)}) copy-start(bf16[32,2048]{1,0:T(8,128)(2,1)S(1)} %get-tuple-element.7) | copy-start | bytes 393220
  597.9 0.9 copy-start.7
  599.0 3.2 copy-start.5
Sparse Core Ops, SparseCore 0:
  520.0 57.3 all-gather.1
where the time goes:
time: 611 us; the launch traced here: 610 us
  waiting for transfers between devices  409 us (67%)
  blocking collectives  74.7 us (12%)
  local copies, waits for them, and re-layouts  53.2 us (9%)
  starting transfers between devices  36.3 us (6%)
  matrix products  18.7 us (3%)
  between operations  14.4 us (2%)
    all_to_all x1, waiting for transfers between devices, local(): lax.all_to_all(local_in.reshape(ep_size, features // ep_size, 2 * inner),...  123 us
    all_to_all x1, waiting for transfers between devices, local(): lax.all_to_all(regrouped_in, 'ep', split_axis=0, concat_axis=0, tiled=True)  114 us
    all_to_all x1, blocking collectives, local(): lax.all_to_all(local_out.reshape(ep_size, inner // ep_size, features), 'e...  74.7 us
    all_to_all x1, waiting for transfers between devices, local(): lax.all_to_all(regrouped_out, 'ep', split_axis=0, concat_axis=0, tiled=True)  63.5 us
    all_to_all x2, waiting for transfers between devices, routed_layer(): lax.all_to_all(packed, 'ep', split_axis=0, concat_axis=0, tiled=True)  60.8 us
    all_to_all x2, waiting for transfers between devices, routed_layer(): lax.all_to_all(result.reshape(sources, slot_count, columns), 'ep', split_...  46.9 us
  transfers between devices with their start and end apart: 8, of which 7 were waited for; matrix products, arithmetic and copies ran while one was open for 10% of the time, Pallas kernels for 0%

commit v1 on v0

v1 whole, which is shorter than its diff:
```python
import jax
import jax.numpy as jnp
from jax import lax
from jax.sharding import PartitionSpec as P

TOP = 6
LANES = 128
BF = jnp.bfloat16
F32 = jnp.float32


def rms_norm(hidden, norm_gain):
    values = hidden.astype(F32)
    inverse_rms = lax.rsqrt(jnp.mean(values * values, axis=-1, keepdims=True) + 1e-06)
    return (values * inverse_rms * norm_gain.astype(F32)).astype(BF)


def local(
    tokens_one,
    routes_one,
    gates_one,
    tokens_two,
    routes_two,
    gates_two,
    old_table,
    new_table,
    gate_up,
    down_proj,
    norm_gain,
    kv_weight,
):
    w_in = gate_up[0]
    w_out = down_proj[0]
    ep = lax.axis_size("ep")
    grp = lax.axis_size("grp")
    me = lax.axis_index("ep")
    gi = lax.axis_index("grp")
    rows = tokens_one.shape[0]
    feat = w_in.shape[0]
    inner = w_out.shape[0]
    numbers = jnp.arange(ep, dtype=jnp.int32)
    sources_new = jnp.sum(
        (new_table[:, None] == old_table[None, :]).astype(jnp.int32) * numbers[None, :], axis=1
    )
    new_here = jnp.sum((sources_new == me).astype(jnp.int32) * numbers)

    part_rows = feat // grp
    half_in = lax.dynamic_slice_in_dim(w_in, gi * part_rows, part_rows, 0)
    half_out = lax.dynamic_slice_in_dim(w_out, gi * part_rows, part_rows, 1)
    half_in = half_in.reshape(ep, part_rows // ep, 2 * inner)
    nr = 8
    nc = ep // nr
    half_out = (
        half_out.reshape(nr, inner // nr, nc, part_rows // nc)
        .transpose(0, 2, 1, 3)
        .reshape(ep, inner // nr, part_rows // nc)
    )

    def a2a(x):
        return lax.all_to_all(x, "ep", split_axis=0, concat_axis=0, tiled=True)

    def ext(tok, gat, rou):
        pad = jnp.zeros((rows, LANES - 2 * TOP), BF)
        return jnp.concatenate([tok, gat, rou.astype(BF), pad], axis=1)

    mine = jnp.concatenate(
        [ext(tokens_one, gates_one, routes_one), ext(tokens_two, gates_two, routes_two)], axis=0
    )
    everyone = lax.all_gather(mine, "ep", axis=0, tiled=True)
    act = everyone[:, :feat]
    gat = everyone[:, feat : feat + TOP].astype(F32).reshape(ep, 2, rows, TOP)
    rou = everyone[:, feat + TOP : feat + 2 * TOP].astype(jnp.int32).reshape(ep, 2, rows, TOP)
    target = jnp.stack([me, new_here])[None, :, None, None]
    share = jnp.sum(jnp.where(rou == target, gat, 0.0), axis=-1).reshape(ep * 2 * rows, 1)

    joined = jnp.dot(act, w_in, preferred_element_type=F32)
    hidden = (jax.nn.silu(joined[:, :inner]) * joined[:, inner:]).astype(BF)
    out = jnp.dot(hidden, w_out, preferred_element_type=F32)
    partial = (out * share).astype(BF)
    mix = lax.psum_scatter(partial, "ep", scatter_dimension=0, tiled=True)

    spread_in = a2a(half_in)
    spread_out = a2a(half_out)
    new_in = a2a(spread_in[sources_new])
    new_out = a2a(spread_out[sources_new])
    gate_up_new = new_in.reshape(1, part_rows, 2 * inner)
    down_proj_new = (
        new_out.reshape(nr, nc, inner // nr, part_rows // nc)
        .transpose(0, 2, 1, 3)
        .reshape(1, inner, part_rows)
    )

    own = jnp.concatenate([tokens_one, tokens_two], axis=0)
    hidden_all = (own.astype(F32) + mix.astype(F32)).astype(BF)
    normed = rms_norm(hidden_all, norm_gain)
    kv = jnp.dot(
        normed,
        lax.all_gather(kv_weight, "grp", axis=1, tiled=True),
        preferred_element_type=F32,
    ).astype(BF)
    return (
        hidden_all[:rows],
        kv[:rows],
        hidden_all[rows:],
        kv[rows:],
        gate_up_new,
        down_proj_new,
    )


def solution(mesh):
    tok = P(("grp", "ep"), None)
    return jax.shard_map(
        local,
        mesh=mesh,
        in_specs=(
            tok,
            tok,
            tok,
            tok,
            tok,
            tok,
            P(),
            P(),
            P("ep", None, None),
            P("ep", None, None),
            P(),
            P(None, "grp"),
        ),
        out_specs=(tok, tok, tok, tok, P("ep", "grp", None), P("ep", None, "grp")),
        check_vma=False,
    )
```

time: 611 us -> 303 us (0.50)
  waiting for transfers between devices: 409 us -> 203 us
  blocking collectives: 74.7 us -> 0 us
  local copies, waits for them, and re-layouts: 53.2 us -> 37 us
  starting transfers between devices: 36.3 us -> 21 us
    all_to_all x7 -> x4, waiting for transfers between devices: 409 us -> 203 us  [a2a(): return lax.all_to_all(x, 'ep', split_axis=0, concat_axis=0, tiled=True)]
    all_to_all x1 -> x0, blocking collectives: 74.7 us -> none  [local(): lax.all_to_all(local_out.reshape(ep_size, inner // ep_size, features), 'e...]
    all_to_all x7 -> x4, starting transfers between devices: 36.3 us -> 20.7 us  [a2a(): return lax.all_to_all(x, 'ep', split_axis=0, concat_axis=0, tiled=True)]
    scatter x2 -> x0, local copies, waits for them, and re-layouts: 9.92 us -> none  [routed_layer(): jnp.zeros((ep_size * capacity, features), jnp.bfloat16).at[targets]]
    reshape x11 -> x2, local copies, waits for them, and re-layouts: 19.1 us -> 9.38 us  [the longest x1 4.7 us: local(): half_out.reshape(nr, inner // nr, nc, part_rows // nc).transpose(0, 2, 1, 3)]
    transpose x0 -> x2, local copies, waits for them, and re-layouts: none -> 6.46 us  [the longest x1 3.73 us: local(): down_proj_new = new_out.reshape(nr, nc, inner // nr, part_rows // nc).tra...]
    dot_general x6 -> x2, matrix products: 15.7 us -> 15.7 us  [the longest x1 10.5 us: local(): joined = jnp.dot(act, w_in, preferred_element_type=F32)]
  transfers between devices with their start and end apart: 8 -> 7, of which waited for: 7 -> 4; matrix products, arithmetic and copies ran while one was open for 10% -> 16% of each run, Pallas kernels for 0% -> 0%
where the time goes in v1:
time: 303 us; the launch traced here: 302 us
  waiting for transfers between devices  203 us (67%)
  local copies, waits for them, and re-layouts  37 us (12%)
  starting transfers between devices  21 us (7%)
  matrix products  18.8 us (6%)
  between operations  15.6 us (5%)
  other arithmetic  6.4 us (2%)
    all_to_all x4, waiting for transfers between devices, a2a(): return lax.all_to_all(x, 'ep', split_axis=0, concat_axis=0, tiled=True)  203 us
    all_to_all x4, starting transfers between devices, a2a(): return lax.all_to_all(x, 'ep', split_axis=0, concat_axis=0, tiled=True)  20.7 us
    dot_general x1, matrix products, local(): joined = jnp.dot(act, w_in, preferred_element_type=F32)  10.5 us
  transfers between devices with their start and end apart: 7, of which 4 were waited for; matrix products, arithmetic and copies ran while one was open for 16% of the time, Pallas kernels for 0%

profile of v1, /device:TPU:13, one launch (start us, length us, event | category | flops | bytes accessed | tf_op | source)
XLA Modules:
  0.0 302.2 jit_solution(1208578535021975673)
XLA Ops:
  8.1 0.8 convert_element_type.42
  9.0 0.8 copy.38
  9.8 0.7 convert_element_type.43
  10.6 0.8 copy.40
  11.4 1.0 concatenate.13
  12.4 1.0 concatenate.14
  13.4 0.8 pad_maximum_fusion
  14.2 1.3 constant_dynamic-slice_fusion
  15.4 4.7 %reshape.68 = bf16[8,88,2,512]{3,2,1,0:T(2,128)(2,1)} reshape(bf16[1,704,1024]{2,1,0:T(8,128)(2,1)} %constant_dynamic-slice_fusion) | data formatting | bytes 2883584 | tf_op jit(solution)/shard_map/reshape | solution.py:54
  20.1 2.7 copy.42
  22.9 6.6 %all-to-all-start.2 = ((bf16[16,88,512]{2,1,0:T(8,128)(2,1)}), bf16[16,88,512]{2,1,0:T(8,128)(2,1)}, u32[]{:S(2)}, u32[]{:S(2)}) async-start(bf16[16,88,512]{2,1,0:T(8,128)(2,1)} %bitcast.21), calls=%async_computation.3 | async-start | bytes 2883584 | tf_op jit(solution)/shard_map/all_to_all | solution.py:60
  29.4 3.6 %constant_dynamic-slice_fusion.1 = bf16[1,1024,1408]{2,1,0:T(8,128)(2,1)} fusion(bf16[1,2048,1408]{2,1,0:T(8,128)(2,1)} %param.20, s32[]{:T(128)S(6)} %select_n.21), kind=kLoop, calls=%fused_computation.31 | loop fusion | bytes 5767172 | tf_op jit(solution)/shard_map/dynamic_slice | solution.py:48
  33.0 52.4 %all-to-all-done.2 = bf16[16,88,512]{2,1,0:T(8,128)(2,1)} async-done(((bf16[16,88,512]{2,1,0:T(8,128)(2,1)}), bf16[16,88,512]{2,1,0:T(8,128)(2,1)}, u32[]{:S(2)}, u32[]{:S(2)}) %all-to-all-start.2) | async-done | bytes 1441824 | tf_op jit(solution)/shard_map/all_to_all | solution.py:60
  85.5 4.4 %all-to-all-start = ((bf16[16,64,1408]{2,1,0:T(8,128)(2,1)}), bf16[16,64,1408]{2,1,0:T(8,128)(2,1)}, u32[]{:S(2)}, u32[]{:S(2)}) async-start(bf16[16,64,1408]{2,1,0:T(8,128)(2,1)} %bitcast.20), calls=%async_computation.1 | async-start | bytes 5767168 | tf_op jit(solution)/shard_map/all_to_all | solution.py:60
  90.8 0.7 pad_add_fusion
  91.6 1.4 select_reduce_fusion
  93.1 10.5 %fusion = f32[1024,1408]{1,0:T(8,128)S(1)} fusion(bf16[1,2048,1408]{2,1,0:T(8,128)(2,1)} %param.20, bf16[1024,2176]{1,0:T(8,128)(2,1)} %all-gather.3.cloned.1.call-done), kind=kOutput, calls=%fused_computation.3 | convolution fusion | flops 5905580032 | bytes 15728640 | tf_op jit(solution)/shard_map/dot_general | solution.py:76
  103.5 5.2 %multiply_convert_fusion = bf16[1024,2048]{1,0:T(8,128)(2,1)} fusion(f32[1024]{0:T(1024)S(1)} %select_reduce_fusion, bf16[1,704,2048]{2,1,0:T(8,128)(2,1)S(1)} %copy-done, f32[1024,1408]{1,0:T(8,128)S(1)} %fusion), kind=kOutput, calls=%fused_computation.2 | convolution fusion | flops 2961309696 | bytes 13373440 | tf_op jit(solution)/shard_map/dot_general | solution.py:78
  108.8 3.1 %gather_fusion.1 = bf16[16,88,512]{2,1,0:T(8,128)(2,1)} fusion(bf16[16,88,512]{2,1,0:T(8,128)(2,1)} %all-to-all-done.2, s32[1024]{0:T(1024)S(1)} %pad_clamp_fusion), kind=kCustom, calls=%fused_computation.1 | custom fusion | bytes 2883648 | tf_op jit(solution)/shard_map/gather | solution.py:85
  111.9 59.1 %all-to-all-done = bf16[16,64,1408]{2,1,0:T(8,128)(2,1)} async-done(((bf16[16,64,1408]{2,1,0:T(8,128)(2,1)}), bf16[16,64,1408]{2,1,0:T(8,128)(2,1)}, u32[]{:S(2)}, u32[]{:S(2)}) %all-to-all-start) | async-done | bytes 2883616 | tf_op jit(solution)/shard_map/all_to_all | solution.py:60
  171.0 4.9 %all-to-all-start.3 = ((bf16[16,88,512]{2,1,0:T(8,128)(2,1)}), bf16[16,88,512]{2,1,0:T(8,128)(2,1)}, u32[]{:S(2)}, u32[]{:S(2)}) async-start(bf16[16,88,512]{2,1,0:T(8,128)(2,1)} %gather_fusion.1), calls=%async_computation.4 | async-start | bytes 2883584 | tf_op jit(solution)/shard_map/all_to_all | solution.py:60
  175.9 4.2 %gather_fusion = bf16[16,64,1408]{2,1,0:T(8,128)(2,1)} fusion(bf16[16,64,1408]{2,1,0:T(8,128)(2,1)} %all-to-all-done, s32[1024]{0:T(1024)S(1)} %pad_clamp_fusion), kind=kCustom, calls=%fused_computation | custom fusion | bytes 5767232 | tf_op jit(solution)/shard_map/gather | solution.py:84
  180.1 36.1 %all-to-all-done.3 = bf16[16,88,512]{2,1,0:T(8,128)(2,1)} async-done(((bf16[16,88,512]{2,1,0:T(8,128)(2,1)}), bf16[16,88,512]{2,1,0:T(8,128)(2,1)}, u32[]{:S(2)}, u32[]{:S(2)}) %all-to-all-start.3) | async-done | bytes 1441824 | tf_op jit(solution)/shard_map/all_to_all | solution.py:60
  216.2 4.9 %all-to-all-start.1 = ((bf16[16,64,1408]{2,1,0:T(8,128)(2,1)}), bf16[16,64,1408]{2,1,0:T(8,128)(2,1)}, u32[]{:S(2)}, u32[]{:S(2)}) async-start(bf16[16,64,1408]{2,1,0:T(8,128)(2,1)} %gather_fusion), calls=%async_computation.2 | async-start | bytes 5767168 | tf_op jit(solution)/shard_map/all_to_all | solution.py:60
  221.7 3.7 %copy.43 = bf16[8,88,2,512]{3,2,1,0:T(2,128)(2,1)} copy(bf16[8,88,2,512]{3,1,2,0:T(8,128)(2,1)} %bitcast.11) | data formatting | bytes 2883584 | tf_op jit(solution)/shard_map/transpose | solution.py:89
  225.5 4.7 %reshape.71 = bf16[1,704,1024]{2,1,0:T(8,128)(2,1)} reshape(bf16[8,88,2,512]{3,2,1,0:T(2,128)(2,1)} %copy.43) | data formatting | bytes 2883584 | tf_op jit(solution)/shard_map/reshape | solution.py:90
  230.1 55.3 %all-to-all-done.1 = bf16[16,64,1408]{2,1,0:T(8,128)(2,1)} async-done(((bf16[16,64,1408]{2,1,0:T(8,128)(2,1)}), bf16[16,64,1408]{2,1,0:T(8,128)(2,1)}, u32[]{:S(2)}, u32[]{:S(2)}) %all-to-all-start.1) | async-done | bytes 2883616 | tf_op jit(solution)/shard_map/all_to_all | solution.py:60
  285.5 1.1 fusion.7
  286.7 0.7 fusion.16
  287.4 3.1 %convolution_convert_fusion = bf16[64,1024]{1,0:T(8,128)(2,1)S(1)} fusion(bf16[2048,1024]{1,0:T(8,128)(2,1)} %all-gather.5.cloned.1.call-done, bf16[64,2048]{1,0:T(8,128)(2,1)S(1)} %get-tuple-element.7, f32[2048]{0:T(1024)S(1)} %convert_element_type.51, f32[64]{0:T(128)S(1)} %add_rsqrt_fusion), kind=kOutput, calls=%fused_computation.10 | convolution fusion | flops 269025280 | bytes 4595968 | tf_op jit(solution)/shard_map/dot_general | solution.py:96
  290.5 0.7 fusion.17
  291.1 3.6 %copy.45 = bf16[1,1024,1408]{2,1,0:T(8,128)(2,1)} copy(bf16[1,1024,1408]{2,1,0:T(8,128)(2,1)} %bitcast.7) | data formatting | bytes 5767168
  (32 shorter events, 1.9 us)
Async XLA Ops:
  8.0 6.1 %copy-start = (bf16[1,704,2048]{2,1,0:T(8,128)(2,1)S(1)}, bf16[1,704,2048]{2,1,0:T(8,128)(2,1)}, u32[]{:S(2)}) copy-start(bf16[1,704,2048]{2,1,0:T(8,128)(2,1)} %param.21) | copy-start | bytes 8650756
  8.0 83.6 %all-gather.3.cloned.1.call-start = ((), (), s32[]{:S(2)}) async-start(), calls=%async_computation.5 | async-start | bytes 4734976 | tf_op jit(solution)/shard_map/all_gather | solution.py:69
  22.9 62.6 %all-to-all-start.2 = ((bf16[16,88,512]{2,1,0:T(8,128)(2,1)}), bf16[16,88,512]{2,1,0:T(8,128)(2,1)}, u32[]{:S(2)}, u32[]{:S(2)}) async-start(bf16[16,88,512]{2,1,0:T(8,128)(2,1)} %bitcast.21), calls=%async_computation.3 | async-start | bytes 2883584 | tf_op jit(solution)/shard_map/all_to_all | solution.py:60
  33.0 56.9 %copy-start.4 = (s32[16]{0:T(128)S(1)}, s32[16]{0:T(128)}, u32[]{:S(2)}) copy-start(s32[16]{0:T(128)} %param.18) | copy-start | bytes 196
  33.0 56.9 %copy-start.5 = (s32[16]{0:T(128)S(1)}, s32[16]{0:T(128)}, u32[]{:S(2)}) copy-start(s32[16]{0:T(128)} %param.19) | copy-start | bytes 196
  85.5 85.5 %all-to-all-start = ((bf16[16,64,1408]{2,1,0:T(8,128)(2,1)}), bf16[16,64,1408]{2,1,0:T(8,128)(2,1)}, u32[]{:S(2)}, u32[]{:S(2)}) async-start(bf16[16,64,1408]{2,1,0:T(8,128)(2,1)} %bitcast.20), calls=%async_computation.1 | async-start | bytes 5767168 | tf_op jit(solution)/shard_map/all_to_all | solution.py:60
  89.9 195.6 %reduce-scatter.2.cloned.1.call-start = ((), (), s32[]{:S(2)}) async-start(), calls=%async_computation.6 | async-start | bytes 4456448 | tf_op jit(solution)/shard_map/reduce_scatter | solution.py:80
  171.0 45.3 %all-to-all-start.3 = ((bf16[16,88,512]{2,1,0:T(8,128)(2,1)}), bf16[16,88,512]{2,1,0:T(8,128)(2,1)}, u32[]{:S(2)}, u32[]{:S(2)}) async-start(bf16[16,88,512]{2,1,0:T(8,128)(2,1)} %gather_fusion.1), calls=%async_computation.4 | async-start | bytes 2883584 | tf_op jit(solution)/shard_map/all_to_all | solution.py:60
  180.1 41.6 %copy-start.3 = (bf16[2048]{0:T(1024)(128)(2,1)S(1)}, bf16[2048]{0:T(1024)(128)(2,1)}, u32[]{:S(2)}) copy-start(bf16[2048]{0:T(1024)(128)(2,1)} %param.22) | copy-start | bytes 12292
  216.2 69.2 %all-to-all-start.1 = ((bf16[16,64,1408]{2,1,0:T(8,128)(2,1)}), bf16[16,64,1408]{2,1,0:T(8,128)(2,1)}, u32[]{:S(2)}, u32[]{:S(2)}) async-start(bf16[16,64,1408]{2,1,0:T(8,128)(2,1)} %gather_fusion), calls=%async_computation.2 | async-start | bytes 5767168 | tf_op jit(solution)/shard_map/all_to_all | solution.py:60
  221.1 66.3 %all-gather.5.cloned.1.call-start = ((), (), s32[]{:S(2)}) async-start(), calls=%async_computation.7 | async-start | bytes 6291456 | tf_op jit(solution)/shard_map/all_gather | solution.py:98
  221.7 63.8 %copy-start.1 = (bf16[32,2048]{1,0:T(8,128)(2,1)S(1)}, bf16[32,2048]{1,0:T(8,128)(2,1)}, u32[]{:S(2)}) copy-start(bf16[32,2048]{1,0:T(8,128)(2,1)} %param.15) | copy-start | bytes 393220
  221.7 63.8 %copy-start.2 = (bf16[32,2048]{1,0:T(8,128)(2,1)S(1)}, bf16[32,2048]{1,0:T(8,128)(2,1)}, u32[]{:S(2)}) copy-start(bf16[32,2048]{1,0:T(8,128)(2,1)} %param.12) | copy-start | bytes 393220
Sparse Core Ops, SparseCore 0:
  14.3 68.3 all-gather.2
  108.9 86.6 reduce-scatter.1
Sparse Core Ops, SparseCore 1:
  223.2 57.2 all-gather.4
